TPU v7x, 256 devices: a whole 4x4x8 slice. The times are simulated.
256 devices in a mesh: row: 16 (over x_lo, z), col: 16 (over x_hi, y, core).
Axes of the slice: x: 4 (x_hi: 2, x_lo: 2; x = x_hi * 2 + x_lo), y: 4, z: 8, core: 2. Of those that a mesh axis runs over, the one named last changes fastest.
Arguments:
- features: bfloat16 [131072, 256], P(('row', 'col')), may hold values from -6 to 6
- self_weight: bfloat16 [256, 256], replicated, may hold values from -0.375 to 0.375
- neigh_weight: bfloat16 [256, 256], replicated, may hold values from -1.5 to 1.5
- tile_coords: int32 [16, 16, 512, 2], P('row', 'col'), may hold values from 0 to 63, as said below
- tile_columns: int32 [16, 16, 512, 8, 128], P('row', 'col'), may hold values from 0 to 128, as said below
- degree: int32 [131072], P(('row', 'col')), may hold values from 12 to 48
- out_grad: bfloat16 [131072, 256], P(('row', 'col')), may hold values from -6 to 6
Outputs:
- output: bfloat16 [131072, 256], P(('row', 'col'))
- feat_grad: bfloat16 [131072, 256], P(('row', 'col'))
- self_grad: float32 [256, 256], replicated
- neigh_grad: float32 [256, 256], replicated
Inputs may be any that keep to these rules, and one draw needn't show every extreme that they name: `tile_coords`: row blocks lie below 4 * 16 and column blocks below 4 * 16. `tile_columns`: entry 128 marks an empty slot. A device's used tiles take its first slots; the remaining slots are all empty; some device uses all 512 slots.
All inputs are finite; a program needn't handle non-finite values.
Results may differ from a plain program's by a relative error of at most 0.0056.
Values may be sent and summed in bfloat16 or wider, within the bound.
A program may use at most 64 MiB of HBM per device.

v0:
```python
import math

import jax
import jax.numpy as jnp
from jax import lax
from jax.sharding import PartitionSpec as P


def build_tiles(column_group, tile_size):
    lanes = jnp.arange(tile_size, dtype=jnp.int32)
    matches = (column_group[..., None] == lanes).astype(jnp.float32)
    return jnp.sum(matches, axis=1).astype(jnp.bfloat16)


def tile_group(partial_value, coord_group, column_group, source, first_block, block_count):
    tile_size = column_group.shape[2]
    dense_tile = build_tiles(column_group, tile_size)
    offset = coord_group[:, 1] - first_block
    inside = ((offset >= 0) & (offset < block_count)).astype(jnp.bfloat16)
    blocks = source[jnp.clip(offset, 0, block_count - 1)]
    product = jnp.einsum(
        "gij,gjf->gif",
        dense_tile * inside[:, None, None],
        blocks,
        preferred_element_type=jnp.float32,
    )
    return partial_value.at[coord_group[:, 0]].add(product)


def forward_pass(coords, columns, source, running, first_block, block_count):

    def forward_advance(partial_value, inputs):
        coord_group, column_group = inputs
        return (
            tile_group(partial_value, coord_group, column_group, source, first_block, block_count),
            None,
        )

    result, _ = lax.scan(forward_advance, running, (coords, columns))
    return result


def backward_pass(coords, columns, target, running):
    tile_size = columns.shape[3]

    def backward_advance(partial_value, inputs):
        coord_group, column_group = inputs
        dense_tile = build_tiles(column_group, tile_size)
        blocks = target[coord_group[:, 0]]
        product = jnp.einsum("gij,gif->gjf", dense_tile, blocks, preferred_element_type=jnp.float32)
        return (partial_value.at[coord_group[:, 1]].add(product), None)

    result, _ = lax.scan(backward_advance, running, (coords, columns))
    return result


def weight_terms(features, mean_feat, g_pre):
    contract = (((0,), (0,)), ((), ()))
    first = lax.dot_general(features, g_pre, contract, preferred_element_type=jnp.float32)
    second = lax.dot_general(mean_feat, g_pre, contract, preferred_element_type=jnp.float32)
    return (first, second)


def shards(features, self_weight, neigh_weight, tile_coords, tile_columns, degree, out_grad):
    tile_size = tile_columns.shape[4]
    width = features.shape[1]
    per_shard = features.shape[0] // tile_size
    row_blocks = per_shard * lax.axis_size("col")
    col_blocks = per_shard * lax.axis_size("row")
    slot_count = tile_coords.shape[2]
    group_size = math.gcd(16, slot_count)
    coords = tile_coords.reshape(slot_count // group_size, group_size, 2)
    columns = tile_columns.reshape(
        slot_count // group_size, group_size, tile_columns.shape[3], tile_size
    )
    start_sum = jnp.zeros((row_blocks, tile_size, width), jnp.float32)
    gathered = lax.all_gather(features, "row", axis=0, tiled=True)
    source = gathered.reshape(col_blocks, tile_size, width)
    partial_sums = forward_pass(coords, columns, source, start_sum, 0, col_blocks)
    summed = lax.psum_scatter(
        partial_sums.reshape(row_blocks * tile_size, width), "col", scatter_dimension=0, tiled=True
    )
    divisor = degree.astype(jnp.float32)[:, None]
    mean_feat = (summed / divisor).astype(jnp.bfloat16)
    pre = jnp.dot(features, self_weight, preferred_element_type=jnp.float32) + jnp.dot(
        mean_feat, neigh_weight, preferred_element_type=jnp.float32
    )
    sigma = jax.nn.sigmoid(pre)
    output = (pre * sigma).astype(jnp.bfloat16)
    g_pre = (out_grad.astype(jnp.float32) * sigma * (1.0 + pre * (1.0 - sigma))).astype(
        jnp.bfloat16
    )
    grad_pair = lax.psum(weight_terms(features, mean_feat, g_pre), ("row", "col"))
    transpose_last = (((1,), (1,)), ((), ()))
    d_mean = lax.dot_general(
        g_pre, neigh_weight, transpose_last, preferred_element_type=jnp.float32
    )
    scaled = (d_mean / divisor).astype(jnp.bfloat16)
    spread = lax.all_gather(scaled, "col", axis=0, tiled=True).reshape(row_blocks, tile_size, width)
    start_back = jnp.zeros((col_blocks, tile_size, width), jnp.float32)
    column_partial = backward_pass(coords, columns, spread, start_back)
    back_sum = lax.psum_scatter(
        column_partial.reshape(col_blocks * tile_size, width),
        "row",
        scatter_dimension=0,
        tiled=True,
    )
    own_term = lax.dot_general(
        g_pre, self_weight, transpose_last, preferred_element_type=jnp.float32
    )
    feat_grad = (own_term + back_sum).astype(jnp.bfloat16)
    return (output, feat_grad, grad_pair[0], grad_pair[1])


def solution(mesh):
    return jax.shard_map(
        shards,
        mesh=mesh,
        in_specs=(
            P(("row", "col"), None),
            P(),
            P(),
            P("row", "col", None, None),
            P("row", "col", None, None, None),
            P(("row", "col")),
            P(("row", "col"), None),
        ),
        out_specs=(P(("row", "col"), None), P(("row", "col"), None), P(), P()),
        check_vma=False,
    )
```

profile of v0, /device:TPU:32, one launch (start us, length us, event | category | flops | bytes accessed | tf_op | source)
XLA Modules:
  0.0 1217.9 jit_solution(1336505912708324213)
XLA Ops:
  9.4 79.1 %all-gather.3.cloned.1.call-done = bf16[8192,256]{1,0:T(8,128)(2,1)} async-done(((bf16[512,256]{1,0:T(8,128)(2,1)}), bf16[8192,256]{1,0:T(8,128)(2,1)}) %all-gather.3.cloned.1.call-update) | async-done | bytes 4194320 | tf_op jit(solution)/shard_map/all_gather | solution.py:77
  92.7 391.6 %while.20 = (s32[]{:T(128)}, f32[64,128,256]{2,1,0:T(8,128)}, s32[32,16,2]{1,2,0:T(2,128)}, s32[32,16,8,128]{3,2,1,0:T(8,128)}, bf16[64,128,256]{2,1,0:T(8,128)(2,1)}, /*index=5*/s32[]{:T(128)}) while((s32[]{:T(128)}, f32[64,128,256]{2,1,0:T(8,128)}, s32[32,16,2]{1,2,0:T(2,128)}, s32[32,16,8,128]{3,2,1,0:T(8,128)}, ...), condition=%wide.region_3.4_spmd, body=%wide.region_0.3_spmd.sunk | while | flops 141034672 | bytes 12784533 | solution.py:39
  100.3 4.5 scatter_fusion
  112.6 4.5 scatter_fusion
  124.8 4.5 scatter_fusion
  149.2 4.6 scatter_fusion
  161.5 4.6 scatter_fusion
  173.8 4.5 scatter_fusion
  186.0 4.6 scatter_fusion
  210.6 4.5 scatter_fusion
  222.8 4.5 scatter_fusion
  235.0 4.6 scatter_fusion
  247.3 4.6 scatter_fusion
  259.6 4.6 scatter_fusion
  296.1 4.5 scatter_fusion
  308.3 4.5 scatter_fusion
  320.5 4.6 scatter_fusion
  332.9 4.6 scatter_fusion
  345.1 4.5 scatter_fusion
  357.3 4.6 scatter_fusion
  369.6 4.5 scatter_fusion
  418.5 4.6 scatter_fusion
  443.0 4.6 scatter_fusion
  455.3 4.6 scatter_fusion
  479.8 4.5 scatter_fusion
  485.5 107.5 %reduce-scatter.3.cloned.1.call-done = f32[512,256]{1,0:T(8,128)} async-done(((f32[8192,256]{1,0:T(8,128)}), f32[512,256]{1,0:T(8,128)}) %reduce-scatter.3.cloned.1.call-update) | async-done | bytes 524304 | tf_op jit(solution)/shard_map/reduce_scatter | solution.py:80
  598.4 57.3 %all-gather.5.cloned.1.call-done = bf16[8192,256]{1,0:T(8,128)(2,1)} async-done(((bf16[512,256]{1,0:T(8,128)(2,1)}), bf16[8192,256]{1,0:T(8,128)(2,1)}) %all-gather.5.cloned.1.call-update) | async-done | bytes 4194320 | tf_op jit(solution)/shard_map/all_gather | solution.py:99
  660.0 450.0 %while.21 = (s32[]{:T(128)}, f32[64,128,256]{2,1,0:T(8,128)}, s32[32,16,2]{1,2,0:T(2,128)}, s32[32,16,8,128]{3,2,1,0:T(8,128)}, bf16[64,128,256]{2,1,0:T(8,128)(2,1)}, /*index=5*/s32[]{:T(128)}) while((s32[]{:T(128)}, f32[64,128,256]{2,1,0:T(8,128)}, s32[32,16,2]{1,2,0:T(2,128)}, s32[32,16,8,128]{3,2,1,0:T(8,128)}, ...), condition=%wide.region_8.9_spmd, body=%wide.region_5.8_spmd.sunk | while | flops 140772448 | bytes 12784405 | solution.py:53
  669.5 4.6 scatter_fusion.1
  697.7 4.5 scatter_fusion.1
  725.8 4.6 scatter_fusion.1
  739.8 4.5 scatter_fusion.1
  768.0 4.6 scatter_fusion.1
  824.1 4.5 scatter_fusion.1
  866.3 4.6 scatter_fusion.1
  908.4 4.6 scatter_fusion.1
  922.5 4.6 scatter_fusion.1
  936.6 4.5 scatter_fusion.1
  950.7 4.5 scatter_fusion.1
  964.7 4.5 scatter_fusion.1
  978.8 4.6 scatter_fusion.1
  1007.0 4.6 scatter_fusion.1
  1021.1 4.6 scatter_fusion.1
  1035.2 4.5 scatter_fusion.1
  1049.3 4.6 scatter_fusion.1
  1063.4 4.5 scatter_fusion.1
  1077.5 4.5 scatter_fusion.1
  1111.8 95.9 %reduce-scatter.5.cloned.1.call-done = f32[512,256]{1,0:T(8,128)} async-done(((f32[8192,256]{1,0:T(8,128)}), f32[512,256]{1,0:T(8,128)}) %reduce-scatter.5.cloned.1.call-update) | async-done | bytes 524304 | tf_op jit(solution)/shard_map/reduce_scatter | solution.py:102
  (539 shorter events, 671.2 us)
Async XLA Ops:
  7.2 587.0 %copy-start = (bf16[256,256]{1,0:T(8,128)(2,1)S(1)}, bf16[256,256]{1,0:T(8,128)(2,1)}, u32[]{:S(2)}) copy-start(bf16[256,256]{1,0:T(8,128)(2,1)} %param.13) | copy-start | bytes 393220
  7.2 81.2 %all-gather.3.cloned.1.call-start = ((), (), s32[]{:S(2)}) async-start(), calls=%async_computation.2 | async-start | bytes 4456448 | tf_op jit(solution)/shard_map/all_gather | solution.py:77
  7.9 585.1 %reduce-scatter.3.cloned.1.call-start = ((), (), s32[]{:S(2)}) async-start(), calls=%async_computation.3 | async-start | bytes 8912896 | tf_op jit(solution)/shard_map/reduce_scatter | solution.py:80
  484.3 0.7 copy-start.4
  484.3 1.0 copy-start.1
  484.3 1.0 copy-start.2
  484.3 109.9 %copy-start.5 = (bf16[512,256]{1,0:T(8,128)(2,1)S(1)}, bf16[512,256]{1,0:T(8,128)(2,1)}, u32[]{:S(2)}) copy-start(bf16[512,256]{1,0:T(8,128)(2,1)} %param.17) | copy-start | bytes 786436
  484.3 171.3 %all-gather.5.cloned.1.call-start = ((), (), s32[]{:S(2)}) async-start(), calls=%async_computation.4 | async-start | bytes 4456448 | tf_op jit(solution)/shard_map/all_gather | solution.py:99
  596.3 513.6 %all-reduce.3.cloned.1.call-start = ((), (), s32[]{:S(2)}) async-start(), calls=%async_computation.6 | async-start | bytes 1048576 | tf_op jit(solution)/shard_map/psum | solution.py:93
  598.4 609.3 %reduce-scatter.5.cloned.1.call-start = ((), (), s32[]{:S(2)}) async-start(), calls=%async_computation.5 | async-start | bytes 8912896 | tf_op jit(solution)/shard_map/reduce_scatter | solution.py:102
  1109.9 97.7 %copy-start.3 = (bf16[256,256]{1,0:T(8,128)(2,1)S(1)}, bf16[256,256]{1,0:T(8,128)(2,1)}, u32[]{:S(2)}) copy-start(bf16[256,256]{1,0:T(8,128)(2,1)} %param.12) | copy-start | bytes 393220
Sparse Core Ops, SparseCore 0:
  9.8 78.5 all-gather.2
  484.5 108.5 reduce-scatter.2
  596.5 59.1 all-gather.4
  661.7 248.3 all-reduce.2
  1110.1 97.5 reduce-scatter.4
where the time goes:
time: 1230 us; the launch traced here: 1220 us
  other arithmetic  502 us (41%)
  waiting for transfers between devices  340 us (28%)
  local copies, waits for them, and re-layouts  290 us (24%)
  matrix products  70.5 us (6%)
  between operations  13.8 us (1%)
    reduce_sum x64, other arithmetic, build_tiles(): return jnp.sum(matches, axis=1).astype(jnp.bfloat16)  209 us
    scatter-add x32, other arithmetic, tile_group(): return partial_value.at[coord_group[:, 0]].add(product)  145 us
    scatter-add x32, other arithmetic, backward_advance(): return (partial_value.at[coord_group[:, 1]].add(product), None)  145 us
    reduce_scatter x1, waiting for transfers between devices, shards(): lax.psum_scatter(partial_sums.reshape(row_blocks * tile_size, width), 'co...  107 us
    reduce_scatter x1, waiting for transfers between devices, shards(): lax.psum_scatter(column_partial.reshape(col_blocks * tile_size, width), '...  95.9 us
    gather x32, local copies, waits for them, and re-layouts, backward_advance(): blocks = target[coord_group[:, 0]]  89.7 us
    gather x32, local copies, waits for them, and re-layouts, tile_group(): blocks = source[jnp.clip(offset, 0, block_count - 1)]  89.6 us
    all_gather x1, waiting for transfers between devices, shards(): gathered = lax.all_gather(features, 'row', axis=0, tiled=True)  79.1 us
  transfers between devices with their start and end apart: 5, of which 4 were waited for; matrix products, arithmetic and copies ran while one was open for 38% of the time, Pallas kernels for 0%

commit v1 on v0

v1 whole, which is shorter than its diff:
```python
import jax
import jax.numpy as jnp
from jax import lax
from jax.experimental import pallas as pl
from jax.experimental.pallas import tpu as pltpu
from jax.sharding import PartitionSpec as P

TILES = 512
GROUP = 4
GROUPS = 176
LANES = 768
BF = jnp.bfloat16
F32 = jnp.float32


def iota(shape, dim):
    return lax.broadcasted_iota(jnp.int32, shape, dim)


def mask_bf16(mask):
    return mask.astype(F32).astype(BF)


def order_kernel(coords_ref, coords_t_ref, out_ref):
    for d in range(2):
        key = coords_ref[:, d : d + 1]
        hot = (key == iota((TILES, 128), 1)).astype(F32)
        earlier = mask_bf16(iota((TILES, TILES), 0) > iota((TILES, TILES), 1))
        rank = jnp.dot(earlier, hot.astype(BF), preferred_element_type=F32)
        count = jnp.sum(hot, axis=0, keepdims=True)
        groups = (count.astype(jnp.int32) + (GROUP - 1)) >> 2
        upper = mask_bf16(iota((128, 128), 0) < iota((128, 128), 1))
        wide = jnp.broadcast_to(groups.astype(F32), (8, 128)).astype(BF)
        start = jnp.dot(wide, upper, preferred_element_type=F32)[0:1]
        place = jnp.sum(hot * (GROUP * start + rank), axis=1, keepdims=True).astype(jnp.int32)
        slot = mask_bf16(place == iota((TILES, LANES), 1))
        t, r = iota((8, TILES), 1), iota((8, TILES), 0)
        own, other = coords_t_ref[d : d + 1, :], coords_t_ref[1 - d : 2 - d, :]
        rows = jnp.where(
            r == 0, t >> 4, jnp.where(r == 1, t & 15, jnp.where(r == 2, own, jnp.where(r == 3, other, 1)))
        )
        got = jnp.dot(rows.astype(F32).astype(BF), slot, preferred_element_type=F32).astype(jnp.int32)
        out_ref[d, 0:1, :] = jnp.where(got[4:5] > 0, got[0:1] * 16 + got[1:2], TILES)
        out_ref[d, 1:2, :] = got[2:3]
        out_ref[d, 2:3, :] = got[3:4]
        out_ref[d, 3:4, 0:128] = jnp.where(groups > 0, start.astype(jnp.int32) + groups - 1, GROUPS)
        out_ref[d, 3:4, 128:LANES] = jnp.zeros((1, LANES - 128), jnp.int32)
        out_ref[d, 4:8, :] = jnp.zeros((4, LANES), jnp.int32)


class Net:
    def __init__(self, send, recv):
        self.send, self.recv, self.ids, self.open = send, recv, {}, []

    def put(self, name, src, dst, device):
        n = self.ids.setdefault(name, len(self.ids))
        copy = pltpu.make_async_remote_copy(
            src_ref=src,
            dst_ref=dst,
            send_sem=self.send.at[n],
            recv_sem=self.recv.at[n],
            device_id=device,
            device_id_type=pl.DeviceIdType.MESH,
        )
        copy.start()
        self.open.append(copy)

    def wait(self, name, dst, device):
        n = self.ids[name]
        pltpu.make_async_remote_copy(
            src_ref=dst,
            dst_ref=dst,
            send_sem=self.send.at[n],
            recv_sem=self.recv.at[n],
            device_id=device,
            device_id_type=pl.DeviceIdType.MESH,
        ).wait_recv()

    def finish(self):
        for copy in self.open:
            copy.wait_send()


N_SEMS = 280


def main_kernel(
    tab, x_ref, sw_ref, nw_ref, cols_ref, deg_ref, og_ref,
    out_ref, fg_ref, sg_ref, ng_ref,
    at, src0, src1, s0, s1, acc, b0, b1, mean_t, g_ref,
    snd1, rcv1, r_py, r_px, r_qx, r_qy,
    t_xa, r_xa, r_z, t_z, t_xb, r_xb,
    w_sum, w_r1, w_2, w_3,
    send, recv,
):
    r, c = lax.axis_index("row"), lax.axis_index("col")
    xl, z = lax.div(r, 8), lax.rem(r, 8)
    core, chip = lax.rem(c, 2), lax.div(c, 2)
    y, xh = lax.rem(chip, 4), lax.div(chip, 4)
    src, s, b = (src0, src1), (s0, s1), (b0, b1)
    net = Net(send, recv)

    def row_of(dx, dz):
        return lax.rem(xl + dx, 2) * 8 + lax.rem(z + (dz + 8), 8)

    def col_of(dx, dy, dc=0):
        return (lax.rem(xh + dx, 2) * 4 + lax.rem(y + dy, 4)) * 2 + lax.rem(core + dc, 2)

    def to_row(dx, dz):
        return {"row": row_of(dx, dz)}

    def to_col(dx, dy, dc=0):
        return {"col": col_of(dx, dy, dc)}

    barrier = pltpu.get_barrier_semaphore()

    def greet(d, _):
        pl.semaphore_signal(
            barrier, inc=1, device_id={"row": lax.rem(r + d, 16)}, device_id_type=pl.DeviceIdType.MESH
        )
        pl.semaphore_signal(
            barrier, inc=1, device_id={"col": lax.rem(c + d, 16)}, device_id_type=pl.DeviceIdType.MESH
        )
        return 0

    lax.fori_loop(1, 16, greet, 0)

    for k in range(4):
        turned = x_ref[128 * k : 128 * k + 128, :].astype(F32).T.astype(BF)
        src0[4 * r + k] = turned[0:128]
        src1[4 * r + k] = turned[128:256]
    for h in range(2):
        s[h][GROUPS] = jnp.zeros((128, 128), BF)
    at[TILES] = jnp.zeros((128, 128), BF)
    acc[...] = jnp.zeros((128, 128), F32)
    pl.semaphore_wait(barrier, 30)

    def block(h, q, dx, dz):
        return src[h].at[pl.ds(4 * row_of(dx, dz) + 2 * q, 2)]

    streams = ((1, 0), (0, 0), (0, 1))

    def hops(h, q, dx):
        return (4, 3) if (h + q + dx) % 2 else (3, 4)

    def ring_send(h, q, dx, step, way):
        if step <= hops(h, q, dx)[way]:
            sign = 1 - 2 * way
            ref = block(h, q, dx, -sign * (step - 1))
            net.put(("ring", h, q, dx, step, way), ref, ref, to_row(0, sign))

    def gather_start(h):
        ref = block(h, 0, 0, 0)
        net.put(("x0", h), ref, ref, to_row(1, 0))
        for way in range(2):
            ring_send(h, 1, 0, 1, way)
        ref = block(h, 1, 0, 0)
        net.put(("x1", h, 0), ref, ref, to_row(1, 0))
        for way in range(2):
            ring_send(h, 0, 0, 1, way)

    def gather_mid(h):
        net.wait(("x0", h), block(h, 0, 1, 0), to_row(1, 0))
        for way in range(2):
            ring_send(h, 0, 1, 1, way)

    def gather_step(h, step):
        for q, dx in streams:
            for way in range(2):
                if step <= hops(h, q, dx)[way]:
                    sign = 1 - 2 * way
                    ref = block(h, q, dx, -sign * step)
                    net.wait(("ring", h, q, dx, step, way), ref, to_row(0, -sign))
                    ring_send(h, q, dx, step + 1, way)
                    if q == 1:
                        net.put(("x1", h, -sign * step), ref, ref, to_row(1, 0))

    def gather_end(h):
        plus, minus = hops(h, 1, 0)
        for dz in range(-plus, minus + 1):
            net.wait(("x1", h, dz), block(h, 1, 1, dz), to_row(1, 0))

    def build(lo, hi):
        def body(t, _):
            slots = cols_ref[t]
            lane = iota((128, 128), 0).astype(jnp.int16)
            total = None
            for n in range(8):
                hit = jnp.broadcast_to(slots[n : n + 1, :], (128, 128)).astype(jnp.int16) == lane
                one = jnp.where(hit, jnp.ones((), BF), jnp.zeros((), BF))
                total = one if total is None else total + one
            at[t] = total
            return 0

        lax.fori_loop(lo, hi, body, 0, unroll=4)

    def multiply(d, h, lo, hi):
        def body(p, last):
            tiles = [at[tab[d, 0, GROUP * p + i]] for i in range(GROUP)]
            sources = [(src, b)[d][h][tab[d, 2, GROUP * p + i]] for i in range(GROUP)]
            key = tab[d, 1, GROUP * p]
            if d == 0:
                left, right = jnp.concatenate(sources, axis=1), jnp.concatenate(tiles, axis=0)
            else:
                left, right = jnp.concatenate(tiles, axis=1), jnp.concatenate(sources, axis=0)
            product = jnp.dot(left, right, preferred_element_type=F32)
            total = jnp.where(key == last, acc[...], 0.0) + product
            acc[...] = total
            s[h][p] = total.astype(BF)
            return key

        first = tab[d, 1, GROUP * (lo - 1)] if lo else jnp.int32(-1)
        lax.fori_loop(lo, hi, body, first, unroll=16)

    def part(d, h, block_id):
        return s[h][tab[d, 3, block_id]].astype(F32)

    def cols_start(h):
        for dx in (1, 0):
            for dy in (1, 3, 2, 0):
                j = dx * 4 + dy
                for k in range(4):
                    snd1[h, j, k] = s[h][tab[0, 3, 4 * col_of(dx, dy, 1) + k]]
                net.put(("core", h, j), snd1.at[h, j], rcv1.at[h, j], to_col(0, 0, 1))

    def cols_second(h):
        for dx in (1, 0):
            for dy in (1, 3, 2, 0):
                j = dx * 4 + dy
                net.wait(("core", h, j), rcv1.at[h, j], to_col(0, 0, 1))
                for k in range(4):
                    rcv1[h, j, k] = (part(0, h, 4 * col_of(dx, dy) + k) + rcv1[h, j, k].astype(F32)).astype(BF)
                if dx == 1:
                    net.put(("qx", h, dy), rcv1.at[h, j, pl.ds(2, 2)], r_qx.at[h, dy], to_col(1, 0))
                if dy:
                    net.put(("py", h, dy, dx), rcv1.at[h, j, pl.ds(0, 2)], r_py.at[h, dy - 1, dx], to_col(0, dy))

    def cols_third(h):
        for dy in (1, 3, 2):
            net.wait(("qx", h, dy), r_qx.at[h, dy], to_col(1, 0))
            r_qx[h, dy] = (rcv1[h, dy, 2:4].astype(F32) + r_qx[h, dy].astype(F32)).astype(BF)
            net.put(("qy", h, dy), r_qx.at[h, dy], r_qy.at[h, dy - 1], to_col(0, dy))
        total = rcv1[h, 4, 0:2].astype(F32)
        for dy in (1, 3, 2):
            net.wait(("py", h, dy, 1), r_py.at[h, dy - 1, 1], to_col(0, 4 - dy))
            total = total + r_py[h, dy - 1, 1].astype(F32)
        snd1[h, 8, 0:2] = total.astype(BF)
        net.put(("px", h), snd1.at[h, 8, pl.ds(0, 2)], r_px.at[h], to_col(1, 0))

    def cols_end(h):
        total = rcv1[h, 0, 0:2].astype(F32)
        for dy in (1, 3, 2):
            net.wait(("py", h, dy, 0), r_py.at[h, dy - 1, 0], to_col(0, 4 - dy))
            total = total + r_py[h, dy - 1, 0].astype(F32)
        net.wait(("px", h), r_px.at[h], to_col(1, 0))
        total = total + r_px[h].astype(F32)
        net.wait(("qx", h, 0), r_qx.at[h, 0], to_col(1, 0))
        second = rcv1[h, 0, 2:4].astype(F32) + r_qx[h, 0].astype(F32)
        for dy in (1, 3, 2):
            net.wait(("qy", h, dy), r_qy.at[h, dy - 1], to_col(0, 4 - dy))
            second = second + r_qy[h, dy - 1].astype(F32)
        for k in range(4):
            value = (total if k < 2 else second)[k % 2]
            mean_t[k, 128 * h : 128 * h + 128, :] = (value / deg_ref[k : k + 1, :].astype(F32)).astype(BF)

    turned_dims = (((1,), (1,)), ((), ()))

    def dense():
        for k in range(4):
            rows = slice(128 * k, 128 * k + 128)
            mean = mean_t[k].astype(F32).T.astype(BF)
            pre = jnp.dot(x_ref[rows, :], sw_ref[...], preferred_element_type=F32)
            pre = pre + jnp.dot(mean, nw_ref[...], preferred_element_type=F32)
            sig = jax.nn.sigmoid(pre)
            out_ref[rows, :] = (pre * sig).astype(BF)
            g = (og_ref[rows, :].astype(F32) * sig * (1.0 + pre * (1.0 - sig))).astype(BF)
            g_ref[k] = g
            d_mean = lax.dot_general(g, nw_ref[...], turned_dims, preferred_element_type=F32)
            divisor = jnp.broadcast_to(deg_ref[k : k + 1, :].astype(F32), (128, 128)).T
            b0[4 * c + k] = (d_mean[:, 0:128] / divisor).astype(BF)
            b1[4 * c + k] = (d_mean[:, 128:256] / divisor).astype(BF)

    def cblock(h, q, dx, dy, dc=0):
        return b[h].at[pl.ds(4 * col_of(dx, dy, dc) + 2 * q, 2)]

    def to_core(h, q, dx, dy):
        ref = cblock(h, q, dx, dy)
        net.put(("bc", h, q, dx, dy), ref, ref, to_col(0, 0, 1))

    def back_start(h):
        ref = cblock(h, 0, 0, 0)
        net.put(("bx0", h), ref, ref, to_col(1, 0))
        ref = cblock(h, 1, 0, 0)
        for dy in (1, 3, 2):
            net.put(("by1", h, dy), ref, ref, to_col(0, dy))
        net.put(("bx1", h, 0), ref, ref, to_col(1, 0))
        ref = cblock(h, 0, 0, 0)
        for dy in (1, 3, 2):
            net.put(("by0", h, 0, dy), ref, ref, to_col(0, dy))
        to_core(h, 0, 0, 0)
        to_core(h, 1, 0, 0)

    def back_mid(h):
        ref = cblock(h, 0, 1, 0)
        net.wait(("bx0", h), ref, to_col(1, 0))
        for dy in (1, 3, 2):
            net.put(("by0", h, 1, dy), ref, ref, to_col(0, dy))
        for dy in (1, 3, 2):
            ref = cblock(h, 1, 0, 4 - dy)
            net.wait(("by1", h, dy), ref, to_col(0, 4 - dy))
            net.put(("bx1", h, dy), ref, ref, to_col(1, 0))
        to_core(h, 0, 1, 0)
        for dy in (1, 3, 2):
            to_core(h, 1, 0, 4 - dy)

    def back_late(h):
        for dy in (1, 3, 2):
            net.wait(("by0", h, 0, dy), cblock(h, 0, 0, 4 - dy), to_col(0, 4 - dy))
            to_core(h, 0, 0, 4 - dy)
        for dy in (0, 1, 3, 2):
            net.wait(("bx1", h, dy), cblock(h, 1, 1, (4 - dy) % 4), to_col(1, 0))
            to_core(h, 1, 1, (4 - dy) % 4)
        for dy in (1, 3, 2):
            net.wait(("by0", h, 1, dy), cblock(h, 0, 1, 4 - dy), to_col(0, 4 - dy))
            to_core(h, 0, 1, 4 - dy)

    def back_end(h):
        for q in range(2):
            for dx in range(2):
                for dy in range(4):
                    net.wait(("bc", h, q, dx, dy), cblock(h, q, dx, dy, 1), to_col(0, 0, 1))

    def rows_start(h):
        for dz in (4, 3, 5, 2, 6, 1, 7, 0):
            for k in range(2):
                t_xa[h, dz, k] = s[h][tab[1, 3, 4 * row_of(1, dz) + 2 + k]]
            net.put(("xa", h, dz), t_xa.at[h, dz], r_xa.at[h, dz], to_row(1, 0))
        for n, (q, dx) in enumerate(streams):
            if q == 0:
                rows_first(h, n)

    def term(h, n, dz):
        q, dx = streams[n]
        dz = dz % 8
        value = [part(1, h, 4 * row_of(dx, dz) + 2 * q + k) for k in range(2)]
        if q == 1:
            value = [value[k] + r_xa[h, dz, k].astype(F32) for k in range(2)]
        return value

    def rows_first(h, n):
        for way in range(2):
            sign = 1 - 2 * way
            far = hops(h, *streams[n])[way]
            if streams[n][0] == 1:
                net.wait(("xa", h, sign * far % 8), r_xa.at[h, sign * far % 8], to_row(1, 0))
            value = term(h, n, sign * far)
            for k in range(2):
                t_z[h, n, way, k] = value[k].astype(BF)
            net.put(("z", h, n, way, 1), t_z.at[h, n, way], r_z.at[h, n, way, 0], to_row(0, sign))

    def rows_second(h):
        rows_first(h, 0)

    def rows_step(h, step):
        for n in (1, 2, 0):
            for way in range(2):
                sign = 1 - 2 * way
                far = hops(h, *streams[n])[way]
                if step >= far:
                    continue
                dz = sign * (far - step)
                if streams[n][0] == 1:
                    net.wait(("xa", h, dz % 8), r_xa.at[h, dz % 8], to_row(1, 0))
                value = term(h, n, dz)
                ref = r_z.at[h, n, way, step - 1]
                net.wait(("z", h, n, way, step), ref, to_row(0, -sign))
                for k in range(2):
                    r_z[h, n, way, step - 1, k] = (
                        value[k] + r_z[h, n, way, step - 1, k].astype(F32)
                    ).astype(BF)
                net.put(("z", h, n, way, step + 1), ref, r_z.at[h, n, way, step], to_row(0, sign))

    def rows_sum(h, n):
        if streams[n][0] == 1:
            net.wait(("xa", h, 0), r_xa.at[h, 0], to_row(1, 0))
        value = term(h, n, 0)
        for way in range(2):
            far = hops(h, *streams[n])[way]
            net.wait(("z", h, n, way, far), r_z.at[h, n, way, far - 1], to_row(0, 2 * way - 1))
            value = [value[k] + r_z[h, n, way, far - 1, k].astype(F32) for k in range(2)]
        return value

    def rows_late(h):
        value = rows_sum(h, 2)
        for k in range(2):
            t_xb[h, k] = value[k].astype(BF)
        net.put(("xb", h), t_xb.at[h], r_xb.at[h], to_row(1, 0))

    def own_term(k, h):
        return lax.dot_general(
            g_ref[k], sw_ref[128 * h : 128 * h + 128, :], turned_dims, preferred_element_type=F32
        )

    def rows_end(h):
        lanes = slice(128 * h, 128 * h + 128)
        value = rows_sum(h, 0)
        for k in range(2):
            fg_ref[128 * (k + 2) : 128 * (k + 3), lanes] = (value[k] + own_term(k + 2, h)).astype(BF)
        value = rows_sum(h, 1)
        net.wait(("xb", h), r_xb.at[h], to_row(1, 0))
        for k in range(2):
            back = value[k] + r_xb[h, k].astype(F32)
            fg_ref[128 * k : 128 * (k + 1), lanes] = (back + own_term(k, h)).astype(BF)

    def weights_start():
        for h in range(2):
            rows = slice(128 * h, 128 * h + 128)
            own = jnp.concatenate([src[h][4 * r + k] for k in range(4)], axis=1)
            mean = jnp.concatenate([mean_t[k, rows, :] for k in range(4)], axis=1)
            g = jnp.concatenate([g_ref[k] for k in range(4)], axis=0)
            first = jnp.dot(own, g, preferred_element_type=F32).reshape(4, 32, 256)
            second = jnp.dot(mean, g, preferred_element_type=F32).reshape(4, 32, 256)
            w_sum[4 * h : 4 * h + 4] = first
            w_sum[8 + 4 * h : 12 + 4 * h] = second
        for d in range(1, 16):
            target = lax.rem(c + d, 16)
            net.put(("w1", d), w_sum.at[target], w_r1.at[d - 1], {"col": target})

    def weights_second():
        total = w_sum[c]
        for d in range(1, 16):
            net.wait(("w1", d), w_r1.at[d - 1], {"col": lax.rem(c + (16 - d), 16)})
            total = total + w_r1[d - 1]
        w_2[r] = total
        for d in range(1, 16):
            net.put(("w2", d), w_2.at[r], w_2.at[r], {"row": lax.rem(r + d, 16)})

    def weights_third():
        for d in range(1, 16):
            source = lax.rem(r + (16 - d), 16)
            net.wait(("w2", d), w_2.at[source], {"row": source})
        total = w_2[0]
        for n in range(1, 16):
            total = total + w_2[n]
        w_3[c] = total
        for d in range(1, 16):
            net.put(("w3", d), w_3.at[c], w_3.at[c], {"col": lax.rem(c + d, 16)})

    def weights_end():
        for d in range(1, 16):
            source = lax.rem(c + (16 - d), 16)
            net.wait(("w3", d), w_3.at[source], {"col": source})
        for n in range(8):
            sg_ref[32 * n : 32 * n + 32, :] = w_3[n]
            ng_ref[32 * n : 32 * n + 32, :] = w_3[8 + n]

    gather_start(0)
    build(0, 64)
    gather_mid(0)
    build(64, 128)
    gather_step(0, 1)
    gather_start(1)
    build(128, 192)
    gather_step(0, 2)
    gather_mid(1)
    build(192, 288)
    gather_step(0, 3)
    build(288, 384)
    gather_step(0, 4)
    gather_step(1, 1)
    build(384, 512)
    gather_end(0)
    multiply(0, 0, 0, 48)
    gather_step(1, 2)
    multiply(0, 0, 48, 112)
    gather_step(1, 3)
    multiply(0, 0, 112, 176)
    gather_step(1, 4)
    cols_start(0)
    gather_end(1)
    multiply(0, 1, 0, 64)
    cols_second(0)
    multiply(0, 1, 64, 128)
    cols_third(0)
    multiply(0, 1, 128, 176)
    cols_start(1)
    cols_end(0)
    cols_second(1)
    cols_third(1)
    cols_end(1)
    dense()
    back_start(0)
    back_start(1)
    weights_start()
    back_mid(0)
    back_late(0)
    back_mid(1)
    back_end(0)
    multiply(1, 0, 0, 80)
    back_late(1)
    multiply(1, 0, 80, 176)
    rows_start(0)
    weights_second()
    back_end(1)
    rows_second(0)
    multiply(1, 1, 0, 48)
    rows_step(0, 1)
    multiply(1, 1, 48, 96)
    rows_step(0, 2)
    multiply(1, 1, 96, 144)
    rows_step(0, 3)
    multiply(1, 1, 144, 176)
    rows_start(1)
    rows_second(1)
    rows_late(0)
    weights_third()
    rows_step(1, 1)
    rows_step(1, 2)
    rows_end(0)
    rows_step(1, 3)
    weights_end()
    rows_late(1)
    rows_end(1)
    net.finish()


def shards(features, self_weight, neigh_weight, tile_coords, tile_columns, degree, out_grad):
    coords = tile_coords.reshape(TILES, 2)
    tab = pl.pallas_call(order_kernel, out_shape=jax.ShapeDtypeStruct((2, 8, LANES), jnp.int32))(coords, coords.T)
    vmem = pl.BlockSpec(memory_space=pltpu.VMEM)
    shape = jax.ShapeDtypeStruct
    return pl.pallas_call(
        main_kernel,
        out_shape=(shape((512, 256), BF), shape((512, 256), BF), shape((256, 256), F32), shape((256, 256), F32)),
        in_specs=[pl.BlockSpec(memory_space=pltpu.SMEM)] + [vmem] * 6,
        out_specs=[vmem] * 4,
        scratch_shapes=[
            pltpu.VMEM((TILES + 1, 128, 128), BF),
            pltpu.VMEM((64, 128, 128), BF),
            pltpu.VMEM((64, 128, 128), BF),
            pltpu.VMEM((GROUPS + 1, 128, 128), BF),
            pltpu.VMEM((GROUPS + 1, 128, 128), BF),
            pltpu.VMEM((128, 128), F32),
            pltpu.VMEM((64, 128, 128), BF),
            pltpu.VMEM((64, 128, 128), BF),
            pltpu.VMEM((4, 256, 128), BF),
            pltpu.VMEM((4, 128, 256), BF),
            pltpu.VMEM((2, 9, 4, 128, 128), BF),
            pltpu.VMEM((2, 8, 4, 128, 128), BF),
            pltpu.VMEM((2, 3, 2, 2, 128, 128), BF),
            pltpu.VMEM((2, 2, 128, 128), BF),
            pltpu.VMEM((2, 4, 2, 128, 128), BF),
            pltpu.VMEM((2, 3, 2, 128, 128), BF),
            pltpu.VMEM((2, 8, 2, 128, 128), BF),
            pltpu.VMEM((2, 8, 2, 128, 128), BF),
            pltpu.VMEM((2, 3, 2, 4, 2, 128, 128), BF),
            pltpu.VMEM((2, 3, 2, 2, 128, 128), BF),
            pltpu.VMEM((2, 2, 128, 128), BF),
            pltpu.VMEM((2, 2, 128, 128), BF),
            pltpu.VMEM((16, 32, 256), F32),
            pltpu.VMEM((15, 32, 256), F32),
            pltpu.VMEM((16, 32, 256), F32),
            pltpu.VMEM((16, 32, 256), F32),
            pltpu.SemaphoreType.DMA((N_SEMS,)),
            pltpu.SemaphoreType.DMA((N_SEMS,)),
        ],
        compiler_params=pltpu.CompilerParams(
            collective_id=0, has_side_effects=True, vmem_limit_bytes=60 * 1024 * 1024
        ),
    )(
        tab,
        features,
        self_weight,
        neigh_weight,
        tile_columns.reshape(TILES, 8, 128),
        degree.reshape(4, 128),
        out_grad,
    )


def solution(mesh):
    return jax.shard_map(
        shards,
        mesh=mesh,
        in_specs=(
            P(("row", "col"), None),
            P(),
            P(),
            P("row", "col", None, None),
            P("row", "col", None, None, None),
            P(("row", "col")),
            P(("row", "col"), None),
        ),
        out_specs=(P(("row", "col"), None), P(("row", "col"), None), P(), P()),
        check_vma=False,
    )
```

time: 1230 us -> 178 us (0.14)
  other arithmetic: 502 us -> 0 us
  waiting for transfers between devices: 340 us -> 0 us
  local copies, waits for them, and re-layouts: 290 us -> 8.22 us
  Pallas kernels: 0 us -> 169 us
  matrix products: 70.5 us -> 0 us
  between operations: 13.8 us -> 0.64 us
    scatter-add x64 -> x0, other arithmetic: 290 us -> none  [the longest x32 145 us: tile_group(): return partial_value.at[coord_group[:, 0]].add(product)]
    reduce_sum x64 -> x0, other arithmetic: 209 us -> none  [build_tiles(): return jnp.sum(matches, axis=1).astype(jnp.bfloat16)]
    reduce_scatter x2 -> x0, waiting for transfers between devices: 203 us -> none  [the longest x1 107 us: shards(): lax.psum_scatter(partial_sums.reshape(row_blocks * tile_size, width), 'co...]
    gather x64 -> x0, local copies, waits for them, and re-layouts: 179 us -> none  [the longest x32 89.7 us: backward_advance(): blocks = target[coord_group[:, 0]]]
    pallas_call x0 -> x2, Pallas kernels: none -> 169 us  [the longest x1 166 us: shards(): pl.pallas_call(main_kernel, out_shape=(shape((512, 256), BF), shape((512,...]
    all_gather x2 -> x0, waiting for transfers between devices: 136 us -> none  [the longest x1 79.1 us: shards(): gathered = lax.all_gather(features, 'row', axis=0, tiled=True)]
    dot_general x70 -> x0, matrix products: 70.5 us -> none  [the longest x32 48.8 us: backward_advance(): jnp.einsum('gij,gif->gjf', dense_tile, blocks, preferred_element_type=jnp...]
    eq x64 -> x0, local copies, waits for them, and re-layouts: 54.2 us -> none  [build_tiles(): matches = (column_group[..., None] == lanes).astype(jnp.float32)]
  transfers between devices with their start and end apart: 5 -> 0, of which waited for: 4 -> 0; matrix products, arithmetic and copies ran while one was open for 38% -> 0% of each run, Pallas kernels for 0% -> 0%
where the time goes in v1:
time: 178 us; the launch traced here: 177 us
  Pallas kernels  169 us (95%)
  local copies, waits for them, and re-layouts  8.22 us (5%)
    pallas_call x1, Pallas kernels, shards(): pl.pallas_call(main_kernel, out_shape=(shape((512, 256), BF), shape((512,...  166 us
    unnamed x4, local copies, waits for them, and re-layouts  6.68 us

profile of v1, /device:TPU:32, one launch (start us, length us, event | category | flops | bytes accessed | tf_op | source)
XLA Modules:
  0.0 177.5 jit_solution(9761684737329666615)
XLA Ops:
  0.6 1.5 copy.11.coords_ref
  2.2 2.8 %shard_map.102.tab = s32[2,8,768]{2,1,0:T(8,128)} custom-call(s32[512,2]{1,0:T(8,128)} %copy.11.coords_ref, s32[2,512]{1,0:T(2,128)} %bitcast.7), custom_call_target="tpu_custom_call" | custom-call | tf_op jit(solution)/shard_map/pallas_call | solution.py:529
  5.0 165.8 %shard_map.103 = (bf16[512,256]{1,0:T(8,128)(2,1)}, bf16[512,256]{1,0:T(8,128)(2,1)}, f32[256,256]{1,0:T(8,128)}, f32[256,256]{1,0:T(8,128)}) custom-call(s32[2,8,768]{2,1,0:T(8,128)} %shard_map.102.tab, bf16[512,256]{1,0:T(8,128)(2,1)} %x_ref.1, bf16[256,256]{1,0:T(8,128)(2,1)} %sw_ref.1, bf16[256,256]{1,0:T(8,128)(2,1)} %nw_ref.1, s32[512,8,128]{2,1,0:T(8,128)} %bitcast.5, ...), custom_call_target="tpu_custom_call" | custom-call | tf_op jit(solution)/shard_map/pallas_call | solution.py:532
  170.8 1.7 copy.16
  172.5 1.7 copy.17
  174.1 1.7 copy.18
  175.8 1.7 copy.19

commit v2 on v1

--- a/solution.py
+++ b/solution.py
@@ -21,21 +21,22 @@
     return mask.astype(F32).astype(BF)
 
 
-def order_kernel(coords_ref, coords_t_ref, out_ref):
+def order_tiles(coords_ref, out_ref):
+    own_lane = iota((TILES, TILES), 0) == iota((TILES, TILES), 1)
+    earlier = mask_bf16(iota((TILES, TILES), 0) > iota((TILES, TILES), 1))
+    upper = mask_bf16(iota((128, 128), 0) < iota((128, 128), 1))
+    t, r = iota((8, TILES), 1), iota((8, TILES), 0)
     for d in range(2):
-        key = coords_ref[:, d : d + 1]
+        own, other = coords_ref[d : d + 1, :], coords_ref[1 - d : 2 - d, :]
+        key = jnp.sum(jnp.where(own_lane, own.astype(F32), 0.0), axis=1, keepdims=True).astype(jnp.int32)
         hot = (key == iota((TILES, 128), 1)).astype(F32)
-        earlier = mask_bf16(iota((TILES, TILES), 0) > iota((TILES, TILES), 1))
         rank = jnp.dot(earlier, hot.astype(BF), preferred_element_type=F32)
         count = jnp.sum(hot, axis=0, keepdims=True)
         groups = (count.astype(jnp.int32) + (GROUP - 1)) >> 2
-        upper = mask_bf16(iota((128, 128), 0) < iota((128, 128), 1))
         wide = jnp.broadcast_to(groups.astype(F32), (8, 128)).astype(BF)
         start = jnp.dot(wide, upper, preferred_element_type=F32)[0:1]
         place = jnp.sum(hot * (GROUP * start + rank), axis=1, keepdims=True).astype(jnp.int32)
         slot = mask_bf16(place == iota((TILES, LANES), 1))
-        t, r = iota((8, TILES), 1), iota((8, TILES), 0)
-        own, other = coords_t_ref[d : d + 1, :], coords_t_ref[1 - d : 2 - d, :]
         rows = jnp.where(
             r == 0, t >> 4, jnp.where(r == 1, t & 15, jnp.where(r == 2, own, jnp.where(r == 3, other, 1)))
         )
@@ -85,13 +86,13 @@
 
 
 def main_kernel(
-    tab, x_ref, sw_ref, nw_ref, cols_ref, deg_ref, og_ref,
+    tab, x_ref, sw_ref, nw_ref, cols_hbm, deg_ref, og_ref,
     out_ref, fg_ref, sg_ref, ng_ref,
     at, src0, src1, s0, s1, acc, b0, b1, mean_t, g_ref,
     snd1, rcv1, r_py, r_px, r_qx, r_qy,
     t_xa, r_xa, r_z, t_z, t_xb, r_xb,
-    w_sum, w_r1, w_2, w_3,
-    send, recv,
+    w_sum, w_col, w_part, w_row, w_z, w_all,
+    cols_ref, local, send, recv,
 ):
     r, c = lax.axis_index("row"), lax.axis_index("col")
     xl, z = lax.div(r, 8), lax.rem(r, 8)
@@ -114,16 +115,12 @@
 
     barrier = pltpu.get_barrier_semaphore()
 
-    def greet(d, _):
-        pl.semaphore_signal(
-            barrier, inc=1, device_id={"row": lax.rem(r + d, 16)}, device_id_type=pl.DeviceIdType.MESH
-        )
-        pl.semaphore_signal(
-            barrier, inc=1, device_id={"col": lax.rem(c + d, 16)}, device_id_type=pl.DeviceIdType.MESH
-        )
-        return 0
-
-    lax.fori_loop(1, 16, greet, 0)
+    partners = [{"row": lax.rem(r + d, 16)} for d in range(1, 16)]
+    partners += [{"col": lax.rem(c + d, 16)} for d in range(1, 16)]
+    for partner in partners:
+        pl.semaphore_signal(barrier, inc=1, device_id=partner, device_id_type=pl.DeviceIdType.MESH)
+    load_cols = pltpu.make_async_copy(cols_hbm, cols_ref, local.at[0])
+    load_cols.start()
 
     for k in range(4):
         turned = x_ref[128 * k : 128 * k + 128, :].astype(F32).T.astype(BF)
@@ -133,7 +130,7 @@
         s[h][GROUPS] = jnp.zeros((128, 128), BF)
     at[TILES] = jnp.zeros((128, 128), BF)
     acc[...] = jnp.zeros((128, 128), F32)
-    pl.semaphore_wait(barrier, 30)
+    pl.semaphore_wait(barrier, len(partners))
 
     def block(h, q, dx, dz):
         return src[h].at[pl.ds(4 * row_of(dx, dz) + 2 * q, 2)]
@@ -164,16 +161,16 @@
         for way in range(2):
             ring_send(h, 0, 1, 1, way)
 
-    def gather_step(h, step):
-        for q, dx in streams:
-            for way in range(2):
-                if step <= hops(h, q, dx)[way]:
-                    sign = 1 - 2 * way
-                    ref = block(h, q, dx, -sign * step)
-                    net.wait(("ring", h, q, dx, step, way), ref, to_row(0, -sign))
-                    ring_send(h, q, dx, step + 1, way)
-                    if q == 1:
-                        net.put(("x1", h, -sign * step), ref, ref, to_row(1, 0))
+    def gather_step(h, step, n):
+        q, dx = streams[n]
+        for way in range(2):
+            if step <= hops(h, q, dx)[way]:
+                sign = 1 - 2 * way
+                ref = block(h, q, dx, -sign * step)
+                net.wait(("ring", h, q, dx, step, way), ref, to_row(0, -sign))
+                ring_send(h, q, dx, step + 1, way)
+                if q == 1:
+                    net.put(("x1", h, -sign * step), ref, ref, to_row(1, 0))
 
     def gather_end(h):
         plus, minus = hops(h, 1, 0)
@@ -331,13 +328,12 @@
                     net.wait(("bc", h, q, dx, dy), cblock(h, q, dx, dy, 1), to_col(0, 0, 1))
 
     def rows_start(h):
+        rows_first(h, 2)
+        rows_first(h, 1)
         for dz in (4, 3, 5, 2, 6, 1, 7, 0):
             for k in range(2):
                 t_xa[h, dz, k] = s[h][tab[1, 3, 4 * row_of(1, dz) + 2 + k]]
             net.put(("xa", h, dz), t_xa.at[h, dz], r_xa.at[h, dz], to_row(1, 0))
-        for n, (q, dx) in enumerate(streams):
-            if q == 0:
-                rows_first(h, n)
 
     def term(h, n, dz):
         q, dx = streams[n]
@@ -361,24 +357,21 @@
     def rows_second(h):
         rows_first(h, 0)
 
-    def rows_step(h, step):
-        for n in (1, 2, 0):
-            for way in range(2):
-                sign = 1 - 2 * way
-                far = hops(h, *streams[n])[way]
-                if step >= far:
-                    continue
-                dz = sign * (far - step)
-                if streams[n][0] == 1:
-                    net.wait(("xa", h, dz % 8), r_xa.at[h, dz % 8], to_row(1, 0))
-                value = term(h, n, dz)
-                ref = r_z.at[h, n, way, step - 1]
-                net.wait(("z", h, n, way, step), ref, to_row(0, -sign))
-                for k in range(2):
-                    r_z[h, n, way, step - 1, k] = (
-                        value[k] + r_z[h, n, way, step - 1, k].astype(F32)
-                    ).astype(BF)
-                net.put(("z", h, n, way, step + 1), ref, r_z.at[h, n, way, step], to_row(0, sign))
+    def rows_step(h, step, n):
+        for way in range(2):
+            sign = 1 - 2 * way
+            far = hops(h, *streams[n])[way]
+            if step >= far:
+                continue
+            dz = sign * (far - step)
+            if streams[n][0] == 1:
+                net.wait(("xa", h, dz % 8), r_xa.at[h, dz % 8], to_row(1, 0))
+            value = term(h, n, dz)
+            ref = r_z.at[h, n, way, step - 1]
+            net.wait(("z", h, n, way, step), ref, to_row(0, -sign))
+            for k in range(2):
+                r_z[h, n, way, step - 1, k] = (value[k] + r_z[h, n, way, step - 1, k].astype(F32)).astype(BF)
+            net.put(("z", h, n, way, step + 1), ref, r_z.at[h, n, way, step], to_row(0, sign))
 
     def rows_sum(h, n):
         if streams[n][0] == 1:
@@ -412,77 +405,119 @@
             back = value[k] + r_xb[h, k].astype(F32)
             fg_ref[128 * k : 128 * (k + 1), lanes] = (back + own_term(k, h)).astype(BF)
 
-    def weights_start():
+    def weights_0():
         for h in range(2):
             rows = slice(128 * h, 128 * h + 128)
             own = jnp.concatenate([src[h][4 * r + k] for k in range(4)], axis=1)
             mean = jnp.concatenate([mean_t[k, rows, :] for k in range(4)], axis=1)
             g = jnp.concatenate([g_ref[k] for k in range(4)], axis=0)
-            first = jnp.dot(own, g, preferred_element_type=F32).reshape(4, 32, 256)
-            second = jnp.dot(mean, g, preferred_element_type=F32).reshape(4, 32, 256)
-            w_sum[4 * h : 4 * h + 4] = first
-            w_sum[8 + 4 * h : 12 + 4 * h] = second
+            w_sum[4 * h : 4 * h + 4] = jnp.dot(own, g, preferred_element_type=F32).reshape(4, 32, 256)
+            w_sum[8 + 4 * h : 12 + 4 * h] = jnp.dot(mean, g, preferred_element_type=F32).reshape(4, 32, 256)
+
+    def weights_1():
         for d in range(1, 16):
             target = lax.rem(c + d, 16)
-            net.put(("w1", d), w_sum.at[target], w_r1.at[d - 1], {"col": target})
-
-    def weights_second():
+            net.put(("w1", d), w_sum.at[target], w_col.at[d - 1], {"col": target})
+
+    def weights_2():
         total = w_sum[c]
         for d in range(1, 16):
-            net.wait(("w1", d), w_r1.at[d - 1], {"col": lax.rem(c + (16 - d), 16)})
-            total = total + w_r1[d - 1]
-        w_2[r] = total
+            net.wait(("w1", d), w_col.at[d - 1], {"col": lax.rem(c + (16 - d), 16)})
+            total = total + w_col[d - 1]
+        for n in range(8):
+            a, e = n // 2, n % 2
+            w_part[n] = total[8 * a : 8 * a + 8, 128 * e : 128 * e + 128]
+        w_row[r] = w_part[z]
         for d in range(1, 16):
-            net.put(("w2", d), w_2.at[r], w_2.at[r], {"row": lax.rem(r + d, 16)})
-
-    def weights_third():
+            target = lax.rem(r + d, 16)
+            net.put(("w2", d), w_part.at[lax.rem(target, 8)], w_row.at[r], {"row": target})
+
+    def weights_3():
         for d in range(1, 16):
             source = lax.rem(r + (16 - d), 16)
-            net.wait(("w2", d), w_2.at[source], {"row": source})
-        total = w_2[0]
+            net.wait(("w2", d), w_row.at[source], {"row": source})
+        total = w_row[0]
         for n in range(1, 16):
-            total = total + w_2[n]
-        w_3[c] = total
+            total = total + w_row[n]
+        w_z[z] = total
+        for dz in range(1, 8):
+            net.put(("w3", dz), w_z.at[z], w_z.at[z], to_row(0, dz))
+
+    def weights_4():
+        for dz in range(1, 8):
+            net.wait(("w3", dz), w_z.at[lax.rem(z + (8 - dz), 8)], to_row(0, 8 - dz))
+        for n in range(8):
+            a, e = n // 2, n % 2
+            w_all[c, 8 * a : 8 * a + 8, 128 * e : 128 * e + 128] = w_z[n]
         for d in range(1, 16):
-            net.put(("w3", d), w_3.at[c], w_3.at[c], {"col": lax.rem(c + d, 16)})
-
-    def weights_end():
+            net.put(("w4", d), w_all.at[c], w_all.at[c], {"col": lax.rem(c + d, 16)})
+
+    def weights_5():
         for d in range(1, 16):
             source = lax.rem(c + (16 - d), 16)
-            net.wait(("w3", d), w_3.at[source], {"col": source})
+            net.wait(("w4", d), w_all.at[source], {"col": source})
         for n in range(8):
-            sg_ref[32 * n : 32 * n + 32, :] = w_3[n]
-            ng_ref[32 * n : 32 * n + 32, :] = w_3[8 + n]
+            sg_ref[32 * n : 32 * n + 32, :] = w_all[n]
+            ng_ref[32 * n : 32 * n + 32, :] = w_all[8 + n]
+
+    def wait_cols():
+        load_cols.wait()
 
     gather_start(0)
-    build(0, 64)
+    wait_cols()
+    build(0, 48)
     gather_mid(0)
-    build(64, 128)
-    gather_step(0, 1)
+    build(48, 80)
+    gather_step(0, 1, 0)
+    build(80, 120)
+    gather_step(0, 1, 1)
+    build(120, 160)
+    gather_step(0, 1, 2)
+    build(160, 200)
+    gather_step(0, 2, 0)
+    build(200, 232)
     gather_start(1)
-    build(128, 192)
-    gather_step(0, 2)
+    gather_step(0, 2, 1)
+    build(232, 264)
+    gather_step(0, 2, 2)
+    build(264, 296)
+    gather_step(0, 3, 0)
+    build(296, 336)
     gather_mid(1)
-    build(192, 288)
-    gather_step(0, 3)
-    build(288, 384)
-    gather_step(0, 4)
-    gather_step(1, 1)
-    build(384, 512)
+    gather_step(0, 3, 1)
+    build(336, 376)
+    gather_step(0, 3, 2)
+    build(376, 416)
+    gather_step(1, 1, 0)
+    build(416, 432)
+    gather_step(1, 1, 1)
+    build(432, 448)
+    gather_step(1, 1, 2)
+    build(448, 464)
+    gather_step(0, 4, 0)
+    build(464, 496)
+    gather_step(0, 4, 1)
+    build(496, 512)
+    gather_step(0, 4, 2)
     gather_end(0)
-    multiply(0, 0, 0, 48)
-    gather_step(1, 2)
-    multiply(0, 0, 48, 112)
-    gather_step(1, 3)
-    multiply(0, 0, 112, 176)
-    gather_step(1, 4)
+    multiply(0, 0, 0, 64)
+    gather_step(1, 2, 0)
+    gather_step(1, 2, 1)
+    gather_step(1, 2, 2)
+    multiply(0, 0, 64, 128)
+    gather_step(1, 3, 0)
+    gather_step(1, 3, 1)
+    gather_step(1, 3, 2)
+    multiply(0, 0, 128, 176)
     cols_start(0)
+    gather_step(1, 4, 0)
+    gather_step(1, 4, 1)
+    gather_step(1, 4, 2)
+    cols_second(0)
     gather_end(1)
-    multiply(0, 1, 0, 64)
-    cols_second(0)
-    multiply(0, 1, 64, 128)
+    multiply(0, 1, 0, 112)
     cols_third(0)
-    multiply(0, 1, 128, 176)
+    multiply(0, 1, 112, 176)
     cols_start(1)
     cols_end(0)
     cols_second(1)
@@ -490,49 +525,66 @@
     cols_end(1)
     dense()
     back_start(0)
-    back_start(1)
-    weights_start()
+    weights_0()
     back_mid(0)
     back_late(0)
+    back_start(1)
+    back_end(0)
+    multiply(1, 0, 0, 48)
     back_mid(1)
-    back_end(0)
-    multiply(1, 0, 0, 80)
+    multiply(1, 0, 48, 128)
     back_late(1)
-    multiply(1, 0, 80, 176)
+    weights_1()
+    multiply(1, 0, 128, 176)
     rows_start(0)
-    weights_second()
     back_end(1)
+    multiply(1, 1, 0, 96)
     rows_second(0)
-    multiply(1, 1, 0, 48)
-    rows_step(0, 1)
-    multiply(1, 1, 48, 96)
-    rows_step(0, 2)
-    multiply(1, 1, 96, 144)
-    rows_step(0, 3)
-    multiply(1, 1, 144, 176)
+    rows_step(0, 1, 2)
+    rows_step(0, 1, 1)
+    multiply(1, 1, 96, 176)
+    weights_2()
     rows_start(1)
+    rows_step(0, 1, 0)
+    rows_step(0, 2, 2)
+    rows_step(0, 2, 1)
     rows_second(1)
+    rows_step(0, 2, 0)
+    weights_3()
+    rows_step(1, 1, 2)
+    rows_step(0, 3, 2)
+    rows_step(1, 1, 1)
+    rows_step(0, 3, 1)
+    rows_step(1, 1, 0)
+    weights_4()
+    rows_step(0, 3, 0)
+    rows_step(1, 2, 2)
+    rows_step(1, 2, 1)
     rows_late(0)
-    weights_third()
-    rows_step(1, 1)
-    rows_step(1, 2)
+    rows_step(1, 2, 0)
+    rows_step(1, 3, 2)
+    rows_step(1, 3, 1)
+    rows_step(1, 3, 0)
     rows_end(0)
-    rows_step(1, 3)
-    weights_end()
     rows_late(1)
+    weights_5()
     rows_end(1)
     net.finish()
 
 
+def hand_on(*refs):
+    for n in range(4):
+        refs[4 + n][...] = refs[n][...]
+
+
 def shards(features, self_weight, neigh_weight, tile_coords, tile_columns, degree, out_grad):
-    coords = tile_coords.reshape(TILES, 2)
-    tab = pl.pallas_call(order_kernel, out_shape=jax.ShapeDtypeStruct((2, 8, LANES), jnp.int32))(coords, coords.T)
     vmem = pl.BlockSpec(memory_space=pltpu.VMEM)
     shape = jax.ShapeDtypeStruct
-    return pl.pallas_call(
+    tab = pl.pallas_call(order_tiles, out_shape=shape((2, 8, LANES), jnp.int32))(tile_coords.reshape(TILES, 2).T)
+    results = pl.pallas_call(
         main_kernel,
         out_shape=(shape((512, 256), BF), shape((512, 256), BF), shape((256, 256), F32), shape((256, 256), F32)),
-        in_specs=[pl.BlockSpec(memory_space=pltpu.SMEM)] + [vmem] * 6,
+        in_specs=[pl.BlockSpec(memory_space=pltpu.SMEM)] + [vmem] * 3 + [pl.BlockSpec(memory_space=pl.ANY)] + [vmem] * 2,
         out_specs=[vmem] * 4,
         scratch_shapes=[
             pltpu.VMEM((TILES + 1, 128, 128), BF),
@@ -559,8 +611,12 @@
             pltpu.VMEM((2, 2, 128, 128), BF),
             pltpu.VMEM((16, 32, 256), F32),
             pltpu.VMEM((15, 32, 256), F32),
+            pltpu.VMEM((8, 8, 128), F32),
+            pltpu.VMEM((16, 8, 128), F32),
+            pltpu.VMEM((8, 8, 128), F32),
             pltpu.VMEM((16, 32, 256), F32),
-            pltpu.VMEM((16, 32, 256), F32),
+            pltpu.VMEM((TILES, 8, 128), jnp.int32),
+            pltpu.SemaphoreType.DMA((1,)),
             pltpu.SemaphoreType.DMA((N_SEMS,)),
             pltpu.SemaphoreType.DMA((N_SEMS,)),
         ],
@@ -576,6 +632,7 @@
         degree.reshape(4, 128),
         out_grad,
     )
+    return pl.pallas_call(hand_on, out_shape=tuple(shape(a.shape, a.dtype) for a in results))(*results)
 
 
 def solution(mesh):

time: 178 us -> 152 us (0.85)
  Pallas kernels: 169 us -> 151 us
  local copies, waits for them, and re-layouts: 8.22 us -> 0 us
    pallas_call x1, Pallas kernels: 166 us -> 146 us  [shards(): pl.pallas_call(main_kernel, out_shape=(shape((512, 256), BF), shape((512,...]
    unnamed x4 -> x0, local copies, waits for them, and re-layouts: 6.68 us -> none
    pallas_call x1 -> x2, Pallas kernels: 2.78 us -> 4.71 us  [the longest x1 2.54 us: shards(): pl.pallas_call(order_tiles, out_shape=shape((2, 8, LANES), jnp.int32))]
where the time goes in v2:
time: 152 us
  Pallas kernels  151 us (99%)
    pallas_call x1, Pallas kernels, shards(): pl.pallas_call(main_kernel, out_shape=(shape((512, 256), BF), shape((512,...  146 us

profile of v2, /device:TPU:32, one launch (start us, length us, event | category | flops | bytes accessed | tf_op | source)
XLA Modules:
  0.0 151.6 jit_solution(12731563492795885234)
XLA Ops:
  0.6 2.5 %shard_map.102.tab = s32[2,8,768]{2,1,0:T(8,128)} custom-call(s32[2,512]{1,0:T(2,128)} %bitcast.6), custom_call_target="tpu_custom_call" | custom-call | tf_op jit(solution)/shard_map/pallas_call | solution.py:583
  3.2 146.3 %shard_map.103 = (bf16[512,256]{1,0:T(8,128)(2,1)}, bf16[512,256]{1,0:T(8,128)(2,1)}, f32[256,256]{1,0:T(8,128)}, f32[256,256]{1,0:T(8,128)}) custom-call(s32[2,8,768]{2,1,0:T(8,128)} %shard_map.102.tab, bf16[512,256]{1,0:T(8,128)(2,1)} %x_ref.1, bf16[256,256]{1,0:T(8,128)(2,1)} %sw_ref.1, bf16[256,256]{1,0:T(8,128)(2,1)} %nw_ref.1, s32[512,8,128]{2,1,0:T(8,128)} %bitcast.5, ...), custom_call_target="tpu_custom_call" | custom-call | tf_op jit(solution)/shard_map/pallas_call | solution.py:584
  149.5 2.2 %shard_map.104 = (bf16[512,256]{1,0:T(8,128)(2,1)}, bf16[512,256]{1,0:T(8,128)(2,1)}, f32[256,256]{1,0:T(8,128)}, f32[256,256]{1,0:T(8,128)}) custom-call(bf16[512,256]{1,0:T(8,128)(2,1)} %get-tuple-element.8.refs_0_, bf16[512,256]{1,0:T(8,128)(2,1)} %get-tuple-element.9.refs_1_, f32[256,256]{1,0:T(8,128)} %get-tuple-element.10.refs_2_, ...), custom_call_target="tpu_custom_call" | custom-call | tf_op jit(solution)/shard_map/pallas_call | solution.py:635
